TPU v7x, 32 devices: a whole 2x2x4 slice. The times are simulated.
32 devices in a mesh: dp: 4 (over y, x), seq: 8 (over z, core).
Axes of the slice: x: 2, y: 2, z: 4, core: 2. Of those that a mesh axis runs over, the one named last changes fastest.
Arguments:
- query: float32 [4, 256, 1024], P('dp', None, 'seq'), may hold values from -6 to 6
- key_in: float32 [4, 256, 1024], P('dp', None, 'seq'), may hold values from -6 to 6
- value: float32 [4, 256, 1024], P('dp', None, 'seq'), may hold values from -6 to 6
- grad_out: float32 [4, 256, 1024], P('dp', None, 'seq'), may hold values from -6 to 6
- filt: float32 [256, 1024], P('seq'), may hold values from -0.1875 to 0.1875
Outputs:
- output: float32 [4, 256, 1024], P('dp', None, 'seq')
- grad_query: float32 [4, 256, 1024], P('dp', None, 'seq')
- grad_key: float32 [4, 256, 1024], P('dp', None, 'seq')
- grad_value: float32 [4, 256, 1024], P('dp', None, 'seq')
- grad_filt: float32 [256, 1024], P('seq')
All inputs are finite; a program needn't handle non-finite values.
Results may differ from a plain program's by a relative error of at most 0.00016.
Values sent between devices are 32-bit elements; how exact they have to be, the bound alone decides.
A program may use at most 64 MiB of HBM per device.

v0:
```python
import math

import jax
import jax.numpy as jnp
from jax import lax
from jax.sharding import PartitionSpec as P

highest = lax.Precision.HIGHEST


def dft_tables(rows, cols, total, sign):
    first = jnp.arange(rows, dtype=jnp.int32)
    second = jnp.arange(cols, dtype=jnp.int32)
    product = first[:, None] * second[None, :] % total
    angles = product.astype(jnp.float32) * (sign * 2.0 * math.pi / total)
    return (jnp.cos(angles), jnp.sin(angles))


def direct_last(real, imag, sign):
    length = real.shape[-1]
    cosine, sine = dft_tables(length, length, length, sign)
    out_real = jnp.einsum("...n,kn->...k", real, cosine, precision=highest) - jnp.einsum(
        "...n,kn->...k", imag, sine, precision=highest
    )
    out_imag = jnp.einsum("...n,kn->...k", imag, cosine, precision=highest) + jnp.einsum(
        "...n,kn->...k", real, sine, precision=highest
    )
    return (out_real, out_imag)


def transform(real, imag, sign):
    length = real.shape[-1]
    rest = 128
    radix = length // rest
    leading = real.shape[:-1]
    real = real.reshape(leading + (radix, rest))
    imag = imag.reshape(leading + (radix, rest))
    cosine, sine = dft_tables(radix, radix, radix, sign)
    part_real = jnp.einsum("kn,...nm->...km", cosine, real, precision=highest) - jnp.einsum(
        "kn,...nm->...km", sine, imag, precision=highest
    )
    part_imag = jnp.einsum("kn,...nm->...km", cosine, imag, precision=highest) + jnp.einsum(
        "kn,...nm->...km", sine, real, precision=highest
    )
    twiddle_cos, twiddle_sin = dft_tables(radix, rest, length, sign)
    turned_real = part_real * twiddle_cos - part_imag * twiddle_sin
    turned_imag = part_real * twiddle_sin + part_imag * twiddle_cos
    inner_real, inner_imag = direct_last(turned_real, turned_imag, sign)
    inner_real = jnp.swapaxes(inner_real, -1, -2).reshape(leading + (length,))
    inner_imag = jnp.swapaxes(inner_imag, -1, -2).reshape(leading + (length,))
    return (inner_real, inner_imag)


def convolve_all(gated, grad_conv, filt):
    length = gated.shape[-1]
    padded = 2 * length
    stacked = jnp.stack([gated[0], filt, grad_conv[0]])
    stacked = jnp.concatenate([stacked, jnp.zeros_like(stacked)], axis=-1)
    spec_real, spec_imag = transform(stacked, jnp.zeros_like(stacked), -1.0)
    g_re, f_re, d_re = (spec_real[0], spec_real[1], spec_real[2])
    g_im, f_im, d_im = (spec_imag[0], spec_imag[1], spec_imag[2])
    prod_real = jnp.stack(
        [f_re * g_re - f_im * g_im, f_re * d_re + f_im * d_im, g_re * d_re + g_im * d_im]
    )
    prod_imag = jnp.stack(
        [f_re * g_im + f_im * g_re, f_re * d_im - f_im * d_re, g_re * d_im - g_im * d_re]
    )
    back_real, back_imag = transform(prod_real, prod_imag, 1.0)
    result = back_real[:, :, :length] / padded
    return (result[0][None], result[1][None], result[2])


def body(query, key_in, value, grad_out, filt):
    batches = lax.axis_size("dp")
    gated, grad_conv = (
        lax.all_to_all(key_in * value, "seq", split_axis=1, concat_axis=2, tiled=True),
        lax.all_to_all(grad_out * query, "seq", split_axis=1, concat_axis=2, tiled=True),
    )
    conv_chan, grad_chan, filt_local = convolve_all(gated, grad_conv, filt)
    conv, grad_gated = (
        lax.all_to_all(conv_chan, "seq", split_axis=2, concat_axis=1, tiled=True),
        lax.all_to_all(grad_chan, "seq", split_axis=2, concat_axis=1, tiled=True),
    )
    output = query * conv
    grad_query = grad_out * conv
    grad_key = grad_gated * value
    grad_value = grad_gated * key_in
    length = filt.shape[1]
    grad_filt = lax.psum(filt_local, "dp") / math.sqrt(batches * length)
    return (output, grad_query, grad_key, grad_value, grad_filt)


def solution(mesh):
    placed = (
        P("dp", None, "seq"),
        P("dp", None, "seq"),
        P("dp", None, "seq"),
        P("dp", None, "seq"),
        P("seq", None),
    )
    return jax.shard_map(
        body,
        mesh=mesh,
        in_specs=placed,
        out_specs=(
            P("dp", None, "seq"),
            P("dp", None, "seq"),
            P("dp", None, "seq"),
            P("dp", None, "seq"),
            P("seq", None),
        ),
        check_vma=False,
    )
```

profile of v0, /device:TPU:0, one launch (start us, length us, event | category | flops | bytes accessed | tf_op | source)
XLA Modules:
  0.0 121.5 jit_solution(3911450936784477306)
XLA Ops:
  7.2 1.7 %mul.496 = f32[1,256,128]{2,1,0:T(8,128)} multiply(f32[1,256,128]{2,1,0:T(8,128)} %param.8, f32[1,256,128]{2,1,0:T(8,128)} %param.5) | non-fusion elementwise | flops 32768 | bytes 393216 | tf_op jit(solution)/shard_map/mul | solution.py:77
  8.8 6.3 %all-to-all-start.1 = ((f32[1,256,128]{2,0,1:T(1,128)}), f32[1,256,128]{2,0,1:T(1,128)S(1)}, u32[]{:S(2)}, u32[]{:S(2)}) async-start(f32[1,256,128]{2,0,1:T(1,128)} %bitcast.4), calls=%async_computation.1 | async-start | bytes 262144 | tf_op jit(solution)/shard_map/all_to_all | solution.py:77
  15.2 1.6 %mul.495 = f32[1,256,128]{2,1,0:T(8,128)} multiply(f32[1,256,128]{2,1,0:T(8,128)} %param.6, f32[1,256,128]{2,1,0:T(8,128)} %param.7) | non-fusion elementwise | flops 32768 | bytes 393216 | tf_op jit(solution)/shard_map/mul | solution.py:76
  16.9 5.1 %all-to-all-done.1 = f32[1,256,128]{2,0,1:T(1,128)S(1)} async-done(((f32[1,256,128]{2,0,1:T(1,128)}), f32[1,256,128]{2,0,1:T(1,128)S(1)}, u32[]{:S(2)}, u32[]{:S(2)}) %all-to-all-start.1) | async-done | bytes 131104 | tf_op jit(solution)/shard_map/all_to_all | solution.py:77
  22.0 3.4 %all-to-all-start = ((f32[1,256,128]{2,0,1:T(1,128)}), f32[1,256,128]{2,0,1:T(1,128)S(1)}, u32[]{:S(2)}, u32[]{:S(2)}) async-start(f32[1,256,128]{2,0,1:T(1,128)} %bitcast), calls=%async_computation | async-start | bytes 262144 | tf_op jit(solution)/shard_map/all_to_all | solution.py:76
  25.4 0.5 fusion.23
  26.0 6.1 %all-to-all-done = f32[1,256,128]{2,0,1:T(1,128)S(1)} async-done(((f32[1,256,128]{2,0,1:T(1,128)}), f32[1,256,128]{2,0,1:T(1,128)S(1)}, u32[]{:S(2)}, u32[]{:S(2)}) %all-to-all-start) | async-done | bytes 131104 | tf_op jit(solution)/shard_map/all_to_all | solution.py:76
  32.3 0.8 fusion.8
  33.1 0.5 fusion.6
  33.7 0.8 fusion.5
  34.5 1.0 fusion.26
  35.5 1.0 fusion.27
  36.6 1.0 fusion.4
  37.6 1.0 fusion.3
  38.9 0.5 copy.60
  39.4 0.3 copy.63
  39.8 0.5 copy.62
  40.3 0.3 copy.65
  40.7 0.5 copy.61
  41.6 0.5 copy.67
  42.4 0.5 copy.68
  43.0 0.3 copy.71
  43.3 0.5 copy.66
  44.2 1.0 fusion.18
  45.3 0.8 fusion.17
  46.1 0.9 fusion.2
  47.0 0.9 fusion.1
  47.9 1.0 fusion.13
  48.9 1.9 %fusion = f32[3,32,128,16]{2,3,1,0:T(8,128)} fusion(f32[3,32,16,128]{3,2,1,0:T(8,128)S(1)} %fusion.13, f32[3,32,16,128]{3,2,1,0:T(8,128)S(1)} %fusion.1, f32[3,32,16,128]{3,2,1,0:T(8,128)S(1)} %fusion.2, f32[16,128]{1,0:T(8,128)S(1)} %get-tuple-element.35, f32[16,128]{1,0:T(8,128)S(1)} %get-tuple-element.36), kind=kOutput, calls=%fused_computation.2 | convolution fusion | flops 303005696 | bytes 3162112 | tf_op jit(solution)/shard_map/...n,kn->...k/dot_general | solution.py:22
  50.8 2.2 %copy.72 = f32[3,32,128,16]{1,3,2,0:T(8,128)S(1)} copy(f32[3,32,128,16]{2,3,1,0:T(8,128)} %fusion) | data formatting | bytes 1572864 | tf_op jit(solution)/shard_map/sub | solution.py:22
  53.1 0.9 slice_bitcast_fusion
  54.0 0.5 broadcast.184
  54.5 1.9 %reduce.2 = f32[1024,32]{1,0:T(8,128)S(1)} reduce(f32[1024,1,32]{2,1,0:T(1,128)S(1)} %bitcast.135, f32[]{:T(128)} %broadcast.184), dimensions={1}, to_apply=%bitcast.114.reduce_sub_computation | reduce | bytes 262148
  56.5 0.9 reshape.379
  57.4 3.4 %all-to-all-start.3 = ((f32[8,1,4096]{2,1,0:T(1,128)}), f32[8,1,4096]{2,1,0:T(1,128)S(1)}, u32[]{:S(2)}, u32[]{:S(2)}) async-start(f32[8,1,4096]{2,1,0:T(1,128)} %reshape.379), calls=%async_computation.3 | async-start | bytes 262144 | tf_op jit(solution)/shard_map/all_to_all | solution.py:82
  60.8 1.9 %reduce = f32[1024,32]{1,0:T(8,128)S(1)} reduce(f32[1024,1,32]{2,1,0:T(1,128)S(1)} %bitcast.134, f32[]{:T(128)} %broadcast.184), dimensions={1}, to_apply=%bitcast.112.reduce_sub_computation | reduce | bytes 262148
  62.7 0.9 reshape.377
  63.6 34.9 %all-reduce.3.cloned.1.call-done = f32[32,1024]{0,1:T(8,128)} async-done(((f32[32,1024]{0,1:T(8,128)}), f32[32,1024]{0,1:T(8,128)}) %all-reduce.3.cloned.1.call-update) | async-done | bytes 131088 | tf_op jit(solution)/shard_map/psum | solution.py:89
  98.5 1.1 broadcast_multiply_fusion
  99.6 0.8 copy.77
  100.5 4.6 %all-to-all-start.2 = ((f32[8,1,4096]{2,1,0:T(1,128)}), f32[8,1,4096]{2,1,0:T(1,128)S(1)}, u32[]{:S(2)}, u32[]{:S(2)}) async-start(f32[8,1,4096]{2,1,0:T(1,128)} %reshape.377), calls=%async_computation.2 | async-start | bytes 262144 | tf_op jit(solution)/shard_map/all_to_all | solution.py:81
  105.1 1.0 reduce.3
  106.0 0.9 reshape.380
  107.2 0.7 bitcast_multiply_fusion
  107.9 4.0 %all-to-all-done.2 = f32[8,1,4096]{2,1,0:T(1,128)S(1)} async-done(((f32[8,1,4096]{2,1,0:T(1,128)}), f32[8,1,4096]{2,1,0:T(1,128)S(1)}, u32[]{:S(2)}, u32[]{:S(2)}) %all-to-all-start.2) | async-done | bytes 131104 | tf_op jit(solution)/shard_map/all_to_all | solution.py:81
  111.9 1.0 reduce.1
  112.8 0.9 reshape.378
  113.9 0.7 bitcast_multiply_fusion.2
  (27 shorter events, 2.1 us)
Async XLA Ops:
  7.2 24.9 %copy-start.4 = (f32[32,1024]{1,0:T(8,128)S(1)}, f32[32,1024]{1,0:T(8,128)}, u32[]{:S(2)}) copy-start(f32[32,1024]{1,0:T(8,128)} %param.9) | copy-start | bytes 393220
  8.8 13.1 %all-to-all-start.1 = ((f32[1,256,128]{2,0,1:T(1,128)}), f32[1,256,128]{2,0,1:T(1,128)S(1)}, u32[]{:S(2)}, u32[]{:S(2)}) async-start(f32[1,256,128]{2,0,1:T(1,128)} %bitcast.4), calls=%async_computation.1 | async-start | bytes 262144 | tf_op jit(solution)/shard_map/all_to_all | solution.py:77
  22.0 10.1 %all-to-all-start = ((f32[1,256,128]{2,0,1:T(1,128)}), f32[1,256,128]{2,0,1:T(1,128)S(1)}, u32[]{:S(2)}, u32[]{:S(2)}) async-start(f32[1,256,128]{2,0,1:T(1,128)} %bitcast), calls=%async_computation | async-start | bytes 262144 | tf_op jit(solution)/shard_map/all_to_all | solution.py:76
  25.3 73.2 %all-reduce.3.cloned.1.call-start = ((), (), s32[]{:S(2)}) async-start(), calls=%async_computation.4 | async-start | bytes 1048576 | tf_op jit(solution)/shard_map/psum | solution.py:89
  57.4 43.1 %all-to-all-start.3 = ((f32[8,1,4096]{2,1,0:T(1,128)}), f32[8,1,4096]{2,1,0:T(1,128)S(1)}, u32[]{:S(2)}, u32[]{:S(2)}) async-start(f32[8,1,4096]{2,1,0:T(1,128)} %reshape.379), calls=%async_computation.3 | async-start | bytes 262144 | tf_op jit(solution)/shard_map/all_to_all | solution.py:82
  63.6 43.5 %copy-start = (f32[1,256,128]{2,1,0:T(8,128)S(1)}, f32[1,256,128]{2,1,0:T(8,128)}, u32[]{:S(2)}) copy-start(f32[1,256,128]{2,1,0:T(8,128)} %param.6) | copy-start | bytes 393220
  63.6 43.5 %copy-start.1 = (f32[1,256,128]{2,1,0:T(8,128)S(1)}, f32[1,256,128]{2,1,0:T(8,128)}, u32[]{:S(2)}) copy-start(f32[1,256,128]{2,1,0:T(8,128)} %param.7) | copy-start | bytes 393220
  100.5 11.4 %all-to-all-start.2 = ((f32[8,1,4096]{2,1,0:T(1,128)}), f32[8,1,4096]{2,1,0:T(1,128)S(1)}, u32[]{:S(2)}, u32[]{:S(2)}) async-start(f32[8,1,4096]{2,1,0:T(1,128)} %reshape.377), calls=%async_computation.2 | async-start | bytes 262144 | tf_op jit(solution)/shard_map/all_to_all | solution.py:81
  107.0 7.0 %copy-start.2 = (f32[1,256,128]{2,1,0:T(8,128)S(1)}, f32[1,256,128]{2,1,0:T(8,128)}, u32[]{:S(2)}) copy-start(f32[1,256,128]{2,1,0:T(8,128)} %param.8) | copy-start | bytes 393220
  107.0 6.9 %copy-start.3 = (f32[1,256,128]{2,1,0:T(8,128)S(1)}, f32[1,256,128]{2,1,0:T(8,128)}, u32[]{:S(2)}) copy-start(f32[1,256,128]{2,1,0:T(8,128)} %param.5) | copy-start | bytes 393220
Sparse Core Ops, SparseCore 0:
  54.1 44.3 all-reduce.2
where the time goes:
time: 122 us
  waiting for transfers between devices  50 us (41%)
  starting transfers between devices  17.7 us (15%)
  between operations  14.4 us (12%)
  local copies, waits for them, and re-layouts  13.9 us (11%)
  matrix products  13.3 us (11%)
  other arithmetic  12.1 us (10%)
    psum x1, waiting for transfers between devices, body(): grad_filt = lax.psum(filt_local, 'dp') / math.sqrt(batches * length)  34.9 us
    all_to_all x1, starting transfers between devices, body(): lax.all_to_all(grad_out * query, 'seq', split_axis=1, concat_axis=2, tile...  6.33 us
    all_to_all x1, waiting for transfers between devices, body(): lax.all_to_all(key_in * value, 'seq', split_axis=1, concat_axis=2, tiled=...  6.06 us
    unnamed x17, local copies, waits for them, and re-layouts  5.19 us
    all_to_all x1, waiting for transfers between devices, body(): lax.all_to_all(grad_out * query, 'seq', split_axis=1, concat_axis=2, tile...  5.08 us
    all_to_all x1, starting transfers between devices, body(): lax.all_to_all(conv_chan, 'seq', split_axis=2, concat_axis=1, tiled=True)  4.61 us
    all_to_all x1, waiting for transfers between devices, body(): lax.all_to_all(conv_chan, 'seq', split_axis=2, concat_axis=1, tiled=True)  3.95 us
    unnamed x2, other arithmetic  3.89 us
  transfers between devices with their start and end apart: 5, of which 4 were waited for; matrix products, arithmetic and copies ran while one was open for 11% of the time, Pallas kernels for 0%

commit v1 on v0

v1 whole, which is shorter than its diff:
```python
import functools
import math

import jax
import jax.numpy as jnp
import ml_dtypes
import numpy as np
from jax import lax
from jax.experimental import pallas as pl
from jax.experimental.pallas import tpu as pltpu
from jax.sharding import PartitionSpec as P

MESH = pl.DeviceIdType.MESH
BLOCK = 128
CHUNK = 8
UNROLL = 8


def tables():
    place = np.arange(BLOCK, dtype=np.float64)
    angle = np.pi * place[:, None] * (2.0 * place[None, :] + 1.0) / (2 * BLOCK)
    ahead = np.concatenate([np.cos(angle), -np.sin(angle)], axis=1)
    back = ahead.T / BLOCK

    def split(table):
        high = table.astype(ml_dtypes.bfloat16)
        low = (table - high.astype(np.float64)).astype(ml_dtypes.bfloat16)
        return (high, low)

    return split(ahead) + split(back)


def dot3(x, high, low):
    x_high = x.astype(jnp.bfloat16)
    x_low = (x - x_high.astype(jnp.float32)).astype(jnp.bfloat16)
    dot = functools.partial(jnp.dot, preferred_element_type=jnp.float32)
    return dot(x_high, high) + (dot(x_low, high) + dot(x_high, low))


def fold(low, high, step, carry):
    if isinstance(low, int) and isinstance(high, int):
        for at in range(low, high):
            carry = step(at, carry)
        return carry
    return lax.fori_loop(low, high, step, carry)


def each(count, step):
    if count <= UNROLL:
        for at in range(count):
            step(at)
    else:

        @pl.loop(0, count)
        def _(at):
            step(at)


def kernel(
    n, nd, ch, cc, scale,
    q_hbm, k_hbm, v_hbm, g_hbm, f_hbm, wh_hbm, wl_hbm, ah_hbm, al_hbm,
    out_q, out_g, out_k, out_v, out_f,
    q, k, v, g, f, wh, wl, ah, al,
    send, recv, fs, xs, hs, zs, ret, back, fb,
    load_sem, s_sem, r_sem, bs_sem, br_sem, fs_sem, fr_sem,
):
    me = lax.axis_index("seq")
    row = lax.axis_index("dp")
    chunks = ch // cc
    offsets = sorted(range(1, n), key=lambda o: -min(o, n - o))

    loads = [
        pltpu.make_async_copy(src, dst, load_sem.at[at])
        for at, (src, dst) in enumerate(
            [
                (k_hbm.at[0], k), (v_hbm.at[0], v), (q_hbm.at[0], q), (g_hbm.at[0], g),
                (f_hbm, f), (wh_hbm, wh), (wl_hbm, wl), (ah_hbm, ah), (al_hbm, al),
            ]
        )
    ]
    for load in loads:
        load.start()

    barrier = pltpu.get_barrier_semaphore()
    for o in range(1, n):
        pl.semaphore_signal(
            barrier, inc=1, device_id={"seq": lax.rem(me + o, n)}, device_id_type=MESH
        )
    for o in range(1, nd):
        pl.semaphore_signal(
            barrier, inc=1, device_id={"dp": lax.rem(row + o, nd)}, device_id_type=MESH
        )

    for load in loads[:4]:
        load.wait()

    def stage(c):
        for p in range(n):
            rows = pl.ds(p * ch + c * cc, cc)
            send[p, c, 0] = k[rows, :] * v[rows, :]
            send[p, c, 1] = g[rows, :] * q[rows, :]
        recv[c, me] = send[me, c]

    def out_copy(c, o):
        to = lax.rem(me + o, n)
        return pltpu.make_async_remote_copy(
            src_ref=send.at[to, c],
            dst_ref=recv.at[c, me],
            send_sem=s_sem.at[c, o - 1],
            recv_sem=r_sem.at[c, o - 1],
            device_id={"seq": to},
            device_id_type=MESH,
        )

    def back_copy(c, o):
        to = lax.rem(me + o, n)
        return pltpu.make_async_remote_copy(
            src_ref=ret.at[c, to],
            dst_ref=back.at[me, c],
            send_sem=bs_sem.at[c, o - 1],
            recv_sem=br_sem.at[c, o - 1],
            device_id={"seq": to},
            device_id_type=MESH,
        )

    def filt_copy(c, o):
        return pltpu.make_async_remote_copy(
            src_ref=fb.at[row, c],
            dst_ref=fb.at[row, c],
            send_sem=fs_sem.at[c, o - 1],
            recv_sem=fr_sem.at[c, o - 1],
            device_id={"dp": lax.rem(row + o, nd)},
            device_id_type=MESH,
        )

    for c in range(chunks):
        stage(c)
        if c == 0:
            pl.semaphore_wait(barrier, n - 1 + nd - 1)
        for o in offsets:
            out_copy(c, o).start()

    for load in loads[4:]:
        load.wait()

    sign = (1 - 2 * (lax.broadcasted_iota(jnp.int32, (1, BLOCK), 1) % 2)).astype(jnp.float32)

    last = None
    for d in range(n):
        spec = dot3(f[:, d * BLOCK : (d + 1) * BLOCK], wh[...], wl[...])
        real, imag = spec[:, :BLOCK], spec[:, BLOCK:]
        if last is None:
            fs[0, d], fs[1, d] = real, imag
        else:
            fs[0, d] = real - sign * last[1]
            fs[1, d] = imag + sign * last[0]
        last = (real, imag)

    zero = jnp.zeros((cc, BLOCK), jnp.float32)

    for c in range(chunks):
        part = pl.ds(c * cc, cc)
        for o in offsets:
            out_copy(c, o).wait_recv()
        spec = dot3(recv[c].reshape(n * 2 * cc, BLOCK), wh[...], wl[...])
        for j in range(n):
            for a in range(2):
                rows = slice((2 * j + a) * cc, (2 * j + a + 1) * cc)
                xs[a, 0, j] = spec[rows, :BLOCK]
                xs[a, 1, j] = spec[rows, BLOCK:]

        def conv_block(i):
            def step(j, carry):
                fr, fi = fs[0, i - j, part], fs[1, i - j, part]
                gr, gi = xs[0, 0, j], xs[0, 1, j]
                return (carry[0] + (fr * gr - fi * gi), carry[1] + (fr * gi + fi * gr))

            real, imag = fold(0, i + 1, step, (zero, zero))
            zs[0, i, :, :BLOCK] = real
            zs[0, i, :, BLOCK:] = imag

        def grad_block(j):
            def step(i, carry):
                fr, fi = fs[0, i - j, part], fs[1, i - j, part]
                dr, di = xs[1, 0, i], xs[1, 1, i]
                return (carry[0] + (fr * dr + fi * di), carry[1] + (fr * di - fi * dr))

            real, imag = fold(j, n, step, (zero, zero))
            zs[1, j, :, :BLOCK] = real
            zs[1, j, :, BLOCK:] = imag

        def filt_block(d):
            def step(j, carry):
                gr, gi = xs[0, 0, j], xs[0, 1, j]
                dr, di = xs[1, 0, j + d], xs[1, 1, j + d]
                return (carry[0] + (gr * dr + gi * di), carry[1] + (gr * di - gi * dr))

            real, imag = fold(0, n - d, step, (zero, zero))
            hs[0, d] = real
            hs[1, d] = imag

        each(n, conv_block)
        each(n, grad_block)
        time = dot3(zs[0:2].reshape(2 * n * cc, 2 * BLOCK), ah[...], al[...])
        for a in range(2):
            for i in range(n):
                at = (a * n + i) * cc
                ret[c, i, a] = time[at : at + cc]
        for o in offsets:
            back_copy(c, o).start()
        back[me, c] = ret[c, me]

        each(n, filt_block)
        for d in range(n):
            real, imag = hs[0, d], hs[1, d]
            if d + 1 < n:
                real, imag = real + sign * hs[1, d + 1], imag - sign * hs[0, d + 1]
            zs[2, d, :, :BLOCK] = real
            zs[2, d, :, BLOCK:] = imag
        time = dot3(zs[2].reshape(n * cc, 2 * BLOCK), ah[...], al[...])
        for d in range(n):
            fb[row, c, d] = time[d * cc : (d + 1) * cc]
        for o in range(1, nd):
            filt_copy(c, o).start()

    for c in range(chunks):
        for o in offsets:
            back_copy(c, o).wait_recv()
        for p in range(n):
            rows = pl.ds(p * ch + c * cc, cc)
            conv, grad = back[p, c, 0], back[p, c, 1]
            out_q[0, rows, :] = q[rows, :] * conv
            out_g[0, rows, :] = g[rows, :] * conv
            out_k[0, rows, :] = grad * v[rows, :]
            out_v[0, rows, :] = grad * k[rows, :]
    for c in range(chunks):
        for o in range(1, nd):
            filt_copy(c, o).wait_recv()
        for d in range(n):
            total = fb[0, c, d]
            for b in range(1, nd):
                total = total + fb[b, c, d]
            out_f[c * cc : (c + 1) * cc, d * BLOCK : (d + 1) * BLOCK] = total * scale
    for c in range(chunks):
        for o in offsets:
            out_copy(c, o).wait_send()
            back_copy(c, o).wait_send()
        for o in range(1, nd):
            filt_copy(c, o).wait_send()


def body(query, key_in, value, grad_out, filt):
    n, nd = lax.axis_size("seq"), lax.axis_size("dp")
    ch, length = filt.shape
    cc = CHUNK
    chunks = ch // cc
    scale = 1.0 / math.sqrt(nd * query.shape[0] * length)
    f32 = jnp.float32
    local = query.shape[1:]
    shape = functools.partial(jax.ShapeDtypeStruct, dtype=f32)
    dma = pltpu.SemaphoreType.DMA
    vmem = functools.partial(pltpu.VMEM, dtype=f32)
    full = tables()
    call = pl.pallas_call(
        functools.partial(kernel, n, nd, ch, cc, scale),
        out_shape=[shape(query.shape)] * 4 + [shape(filt.shape)],
        in_specs=[pl.BlockSpec(memory_space=pl.ANY)] * 9,
        out_specs=[pl.BlockSpec(memory_space=pltpu.VMEM)] * 5,
        scratch_shapes=[vmem(local)] * 4
        + [vmem(filt.shape)]
        + [pltpu.VMEM(t.shape, jnp.bfloat16) for t in full]
        + [
            vmem((n, chunks, 2, cc, BLOCK)),
            vmem((chunks, n, 2, cc, BLOCK)),
            vmem((2, n, ch, BLOCK)),
            vmem((2, 2, n, cc, BLOCK)),
            vmem((2, n, cc, BLOCK)),
            vmem((3, n, cc, 2 * BLOCK)),
            vmem((chunks, n, 2, cc, BLOCK)),
            vmem((n, chunks, 2, cc, BLOCK)),
            vmem((nd, chunks, n, cc, BLOCK)),
            dma((9,)),
            dma((chunks, n - 1)),
            dma((chunks, n - 1)),
            dma((chunks, n - 1)),
            dma((chunks, n - 1)),
            dma((chunks, nd - 1)),
            dma((chunks, nd - 1)),
        ],
        compiler_params=pltpu.CompilerParams(
            collective_id=0, has_side_effects=True, vmem_limit_bytes=24 * 1024 * 1024
        ),
    )
    return tuple(call(query, key_in, value, grad_out, filt, *(jnp.asarray(t) for t in full)))


def solution(mesh):
    spread = P("dp", None, "seq")
    return jax.shard_map(
        body,
        mesh=mesh,
        in_specs=(spread,) * 4 + (P("seq", None),),
        out_specs=(spread,) * 4 + (P("seq", None),),
        check_vma=False,
    )
```

time: 122 us -> 32.9 us (0.27)
  waiting for transfers between devices: 50 us -> 0 us
  Pallas kernels: 0 us -> 20.8 us
  starting transfers between devices: 17.7 us -> 0 us
  between operations: 14.4 us -> 0.66 us
  matrix products: 13.3 us -> 0 us
  other arithmetic: 12.1 us -> 0 us
  local copies, waits for them, and re-layouts: 13.9 us -> 11.1 us
    psum x1 -> x0, waiting for transfers between devices: 34.9 us -> none  [body(): grad_filt = lax.psum(filt_local, 'dp') / math.sqrt(batches * length)]
    pallas_call x0 -> x1, Pallas kernels: none -> 20.8 us  [body(): call(query, key_in, value, grad_out, filt, *(jnp.asarray(t) for t in full))]
    all_to_all x4 -> x0, starting transfers between devices: 17.7 us -> none  [the longest x1 6.33 us: body(): lax.all_to_all(grad_out * query, 'seq', split_axis=1, concat_axis=2, tile...]
    all_to_all x4 -> x0, waiting for transfers between devices: 15.1 us -> none  [the longest x1 6.06 us: body(): lax.all_to_all(key_in * value, 'seq', split_axis=1, concat_axis=2, tiled=...]
    dot_general x14 -> x0, matrix products: 13.3 us -> none  [the longest x2 2.95 us: direct_last(): jnp.einsum('...n,kn->...k', imag, sine, precision=highest)]
    unnamed x17 -> x23, local copies, waits for them, and re-layouts: 5.19 us -> 11.1 us
    sub x7 -> x0, local copies, waits for them, and re-layouts: 4.79 us -> none  [the longest x1 2.16 us: direct_last(): jnp.einsum('...n,kn->...k', real, cosine, precision=highest)]
    mul x4 -> x0, other arithmetic: 4.76 us -> none  [the longest x1 1.67 us: body(): grad_out * query]
  transfers between devices with their start and end apart: 5 -> 0, of which waited for: 4 -> 0; matrix products, arithmetic and copies ran while one was open for 11% -> 0% of each run, Pallas kernels for 0% -> 0%
where the time goes in v1:
time: 32.9 us; the launch traced here: 32.6 us
  Pallas kernels  20.8 us (63%)
  local copies, waits for them, and re-layouts  11.1 us (34%)
  between operations  0.66 us (2%)
    pallas_call x1, Pallas kernels, body(): call(query, key_in, value, grad_out, filt, *(jnp.asarray(t) for t in full))  20.8 us
    unnamed x23, local copies, waits for them, and re-layouts  11.1 us

profile of v1, /device:TPU:0, one launch (start us, length us, event | category | flops | bytes accessed | tf_op | source)
XLA Modules:
  0.0 32.6 jit_solution(10327167330867428505)
XLA Ops:
  0.6 0.0 copy-start
  0.6 0.9 %copy-done = f32[1,256,128]{2,1,0:T(8,128)S(1)} copy-done((f32[1,256,128]{2,1,0:T(8,128)S(1)}, f32[1,256,128]{2,1,0:T(8,128)}, u32[]{:S(2)}) %copy-start) | copy-done | bytes 131096
  1.5 0.0 copy-start.1
  1.5 0.9 %copy-done.1 = f32[1,256,128]{2,1,0:T(8,128)S(1)} copy-done((f32[1,256,128]{2,1,0:T(8,128)S(1)}, f32[1,256,128]{2,1,0:T(8,128)}, u32[]{:S(2)}) %copy-start.1) | copy-done | bytes 131096
  2.4 0.0 copy-start.2
  2.4 0.9 %copy-done.2 = f32[1,256,128]{2,1,0:T(8,128)S(1)} copy-done((f32[1,256,128]{2,1,0:T(8,128)S(1)}, f32[1,256,128]{2,1,0:T(8,128)}, u32[]{:S(2)}) %copy-start.2) | copy-done | bytes 131096
  3.3 0.0 copy-start.3
  3.3 0.9 %copy-done.3 = f32[1,256,128]{2,1,0:T(8,128)S(1)} copy-done((f32[1,256,128]{2,1,0:T(8,128)S(1)}, f32[1,256,128]{2,1,0:T(8,128)}, u32[]{:S(2)}) %copy-start.3) | copy-done | bytes 131096
  4.3 0.0 copy-start.4
  4.3 0.9 %copy-done.4 = f32[32,1024]{1,0:T(8,128)S(1)} copy-done((f32[32,1024]{1,0:T(8,128)S(1)}, f32[32,1024]{1,0:T(8,128)}, u32[]{:S(2)}) %copy-start.4) | copy-done | bytes 131096
  5.2 0.0 copy-start.5
  5.2 0.8 %copy-done.5 = bf16[256,128]{1,0:T(8,128)(2,1)S(1)} copy-done((bf16[256,128]{1,0:T(8,128)(2,1)S(1)}, bf16[256,128]{1,0:T(8,128)(2,1)}, u32[]{:S(2)}) %copy-start.5) | copy-done | bytes 65560
  6.0 0.0 copy-start.6
  6.0 0.8 %copy-done.6 = bf16[256,128]{1,0:T(8,128)(2,1)S(1)} copy-done((bf16[256,128]{1,0:T(8,128)(2,1)S(1)}, bf16[256,128]{1,0:T(8,128)(2,1)}, u32[]{:S(2)}) %copy-start.6) | copy-done | bytes 65560
  6.8 0.0 copy-start.7
  6.8 0.8 %copy-done.7 = bf16[128,256]{1,0:T(8,128)(2,1)S(1)} copy-done((bf16[128,256]{1,0:T(8,128)(2,1)S(1)}, bf16[128,256]{1,0:T(8,128)(2,1)}, u32[]{:S(2)}) %copy-start.7) | copy-done | bytes 65560
  7.7 0.0 copy-start.8
  7.7 0.8 %copy-done.8 = bf16[128,256]{1,0:T(8,128)(2,1)S(1)} copy-done((bf16[128,256]{1,0:T(8,128)(2,1)S(1)}, bf16[128,256]{1,0:T(8,128)(2,1)}, u32[]{:S(2)}) %copy-start.8) | copy-done | bytes 65560
  8.5 20.8 %shard_map.128 = (f32[1,256,128]{2,1,0:T(8,128)S(1)}, f32[1,256,128]{2,1,0:T(8,128)S(1)}, f32[1,256,128]{2,1,0:T(8,128)S(1)}, f32[1,256,128]{2,1,0:T(8,128)S(1)}, f32[32,1024]{1,0:T(8,128)S(1)}) custom-call(f32[1,256,128]{2,1,0:T(8,128)S(1)} %copy-done, f32[1,256,128]{2,1,0:T(8,128)S(1)} %copy-done.1, f32[1,256,128]{2,1,0:T(8,128)S(1)} %copy-done.2, ...), custom_call_target="tpu_custom_call" | custom-call | tf_op jit(solution)/shard_map/pallas_call | solution.py:294
  29.3 0.7 %copy.19 = f32[1,256,128]{2,1,0:T(8,128)} copy(f32[1,256,128]{2,1,0:T(8,128)S(1)} %get-tuple-element.10) | data formatting | bytes 262144
  29.9 0.7 %copy.20 = f32[1,256,128]{2,1,0:T(8,128)} copy(f32[1,256,128]{2,1,0:T(8,128)S(1)} %get-tuple-element.11) | data formatting | bytes 262144
  30.6 0.7 %copy.21 = f32[1,256,128]{2,1,0:T(8,128)} copy(f32[1,256,128]{2,1,0:T(8,128)S(1)} %get-tuple-element.12) | data formatting | bytes 262144
  31.2 0.7 %copy.22 = f32[1,256,128]{2,1,0:T(8,128)} copy(f32[1,256,128]{2,1,0:T(8,128)S(1)} %get-tuple-element.13) | data formatting | bytes 262144
  31.9 0.7 %copy.23 = f32[32,1024]{1,0:T(8,128)} copy(f32[32,1024]{1,0:T(8,128)S(1)} %get-tuple-element.14) | data formatting | bytes 262144
Async XLA Ops:
  0.6 0.9 %copy-start = (f32[1,256,128]{2,1,0:T(8,128)S(1)}, f32[1,256,128]{2,1,0:T(8,128)}, u32[]{:S(2)}) copy-start(f32[1,256,128]{2,1,0:T(8,128)} %q_hbm.1) | copy-start | bytes 393220
  1.5 0.9 %copy-start.1 = (f32[1,256,128]{2,1,0:T(8,128)S(1)}, f32[1,256,128]{2,1,0:T(8,128)}, u32[]{:S(2)}) copy-start(f32[1,256,128]{2,1,0:T(8,128)} %k_hbm.1) | copy-start | bytes 393220
  2.4 0.9 %copy-start.2 = (f32[1,256,128]{2,1,0:T(8,128)S(1)}, f32[1,256,128]{2,1,0:T(8,128)}, u32[]{:S(2)}) copy-start(f32[1,256,128]{2,1,0:T(8,128)} %v_hbm.1) | copy-start | bytes 393220
  3.3 0.9 %copy-start.3 = (f32[1,256,128]{2,1,0:T(8,128)S(1)}, f32[1,256,128]{2,1,0:T(8,128)}, u32[]{:S(2)}) copy-start(f32[1,256,128]{2,1,0:T(8,128)} %g_hbm.1) | copy-start | bytes 393220
  4.3 0.9 %copy-start.4 = (f32[32,1024]{1,0:T(8,128)S(1)}, f32[32,1024]{1,0:T(8,128)}, u32[]{:S(2)}) copy-start(f32[32,1024]{1,0:T(8,128)} %f_hbm.1) | copy-start | bytes 393220
  5.2 0.8 %copy-start.5 = (bf16[256,128]{1,0:T(8,128)(2,1)S(1)}, bf16[256,128]{1,0:T(8,128)(2,1)}, u32[]{:S(2)}) copy-start(bf16[256,128]{1,0:T(8,128)(2,1)} %constant.11.clone.al_hbm) | copy-start | bytes 196612
  6.0 0.8 %copy-start.6 = (bf16[256,128]{1,0:T(8,128)(2,1)S(1)}, bf16[256,128]{1,0:T(8,128)(2,1)}, u32[]{:S(2)}) copy-start(bf16[256,128]{1,0:T(8,128)(2,1)} %constant.10.clone.ah_hbm) | copy-start | bytes 196612
  6.8 0.8 %copy-start.7 = (bf16[128,256]{1,0:T(8,128)(2,1)S(1)}, bf16[128,256]{1,0:T(8,128)(2,1)}, u32[]{:S(2)}) copy-start(bf16[128,256]{1,0:T(8,128)(2,1)} %constant.9.clone.wl_hbm) | copy-start | bytes 196612
  7.7 0.8 %copy-start.8 = (bf16[128,256]{1,0:T(8,128)(2,1)S(1)}, bf16[128,256]{1,0:T(8,128)(2,1)}, u32[]{:S(2)}) copy-start(bf16[128,256]{1,0:T(8,128)(2,1)} %constant.8.clone.wh_hbm) | copy-start | bytes 196612

commit v2 on v1

--- a/solution.py
+++ b/solution.py
@@ -14,6 +14,7 @@
 BLOCK = 128
 CHUNK = 8
 UNROLL = 8
+GRANT = 63 * 1024 * 1024
 
 
 def tables():
@@ -59,10 +60,11 @@
 def kernel(
     n, nd, ch, cc, scale,
     q_hbm, k_hbm, v_hbm, g_hbm, f_hbm, wh_hbm, wl_hbm, ah_hbm, al_hbm,
+    oq_hbm, og_hbm, ok_hbm, ov_hbm, of_hbm,
+    q, k, v, g, f, wh, wl, ah, al,
     out_q, out_g, out_k, out_v, out_f,
-    q, k, v, g, f, wh, wl, ah, al,
     send, recv, fs, xs, hs, zs, ret, back, fb,
-    load_sem, s_sem, r_sem, bs_sem, br_sem, fs_sem, fr_sem,
+    load_sem, save_sem, s_sem, r_sem, bs_sem, br_sem, fs_sem, fr_sem,
 ):
     me = lax.axis_index("seq")
     row = lax.axis_index("dp")
@@ -229,10 +231,21 @@
         for p in range(n):
             rows = pl.ds(p * ch + c * cc, cc)
             conv, grad = back[p, c, 0], back[p, c, 1]
-            out_q[0, rows, :] = q[rows, :] * conv
-            out_g[0, rows, :] = g[rows, :] * conv
-            out_k[0, rows, :] = grad * v[rows, :]
-            out_v[0, rows, :] = grad * k[rows, :]
+            out_q[rows, :] = q[rows, :] * conv
+            out_g[rows, :] = g[rows, :] * conv
+            out_k[rows, :] = grad * v[rows, :]
+            out_v[rows, :] = grad * k[rows, :]
+    saves = [
+        pltpu.make_async_copy(src, dst, save_sem.at[at])
+        for at, (src, dst) in enumerate(
+            [
+                (out_q, oq_hbm.at[0]), (out_g, og_hbm.at[0]), (out_k, ok_hbm.at[0]),
+                (out_v, ov_hbm.at[0]), (out_f, of_hbm),
+            ]
+        )
+    ]
+    for save in saves[:4]:
+        save.start()
     for c in range(chunks):
         for o in range(1, nd):
             filt_copy(c, o).wait_recv()
@@ -241,12 +254,29 @@
             for b in range(1, nd):
                 total = total + fb[b, c, d]
             out_f[c * cc : (c + 1) * cc, d * BLOCK : (d + 1) * BLOCK] = total * scale
+    saves[4].start()
     for c in range(chunks):
         for o in offsets:
             out_copy(c, o).wait_send()
             back_copy(c, o).wait_send()
         for o in range(1, nd):
             filt_copy(c, o).wait_send()
+    for save in saves:
+        save.wait()
+
+
+def writer(*refs):
+    source, target, held = refs[:5], refs[5:10], refs[10:15]
+    load_sem, save_sem = refs[15:]
+    loads = [pltpu.make_async_copy(source[at], held[at], load_sem.at[at]) for at in range(5)]
+    saves = [pltpu.make_async_copy(held[at], target[at], save_sem.at[at]) for at in range(5)]
+    for load in loads:
+        load.start()
+    for load, save in zip(loads, saves):
+        load.wait()
+        save.start()
+    for save in saves:
+        save.wait()
 
 
 def body(query, key_in, value, grad_out, filt):
@@ -264,11 +294,13 @@
     call = pl.pallas_call(
         functools.partial(kernel, n, nd, ch, cc, scale),
         out_shape=[shape(query.shape)] * 4 + [shape(filt.shape)],
-        in_specs=[pl.BlockSpec(memory_space=pl.ANY)] * 9,
-        out_specs=[pl.BlockSpec(memory_space=pltpu.VMEM)] * 5,
+        in_specs=[pl.BlockSpec(memory_space=pltpu.HBM)] * 9,
+        out_specs=[pl.BlockSpec(memory_space=pltpu.HBM)] * 5,
         scratch_shapes=[vmem(local)] * 4
         + [vmem(filt.shape)]
         + [pltpu.VMEM(t.shape, jnp.bfloat16) for t in full]
+        + [vmem(local)] * 4
+        + [vmem(filt.shape)]
         + [
             vmem((n, chunks, 2, cc, BLOCK)),
             vmem((chunks, n, 2, cc, BLOCK)),
@@ -280,6 +312,7 @@
             vmem((n, chunks, 2, cc, BLOCK)),
             vmem((nd, chunks, n, cc, BLOCK)),
             dma((9,)),
+            dma((5,)),
             dma((chunks, n - 1)),
             dma((chunks, n - 1)),
             dma((chunks, n - 1)),
@@ -288,10 +321,19 @@
             dma((chunks, nd - 1)),
         ],
         compiler_params=pltpu.CompilerParams(
-            collective_id=0, has_side_effects=True, vmem_limit_bytes=24 * 1024 * 1024
+            collective_id=0, has_side_effects=True, vmem_limit_bytes=GRANT
         ),
     )
-    return tuple(call(query, key_in, value, grad_out, filt, *(jnp.asarray(t) for t in full)))
+    done = call(query, key_in, value, grad_out, filt, *(jnp.asarray(t) for t in full))
+    store = pl.pallas_call(
+        writer,
+        out_shape=[shape(query.shape)] * 4 + [shape(filt.shape)],
+        in_specs=[pl.BlockSpec(memory_space=pltpu.HBM)] * 5,
+        out_specs=[pl.BlockSpec(memory_space=pltpu.HBM)] * 5,
+        scratch_shapes=[vmem(query.shape)] * 4 + [vmem(filt.shape), dma((5,)), dma((5,))],
+        compiler_params=pltpu.CompilerParams(vmem_limit_bytes=GRANT),
+    )
+    return tuple(store(*done))
 
 
 def solution(mesh):

time: 32.9 us -> 22.9 us (0.70)
  local copies, waits for them, and re-layouts: 11.1 us -> 0 us
  Pallas kernels: 20.8 us -> 22.1 us
    unnamed x23 -> x0, local copies, waits for them, and re-layouts: 11.1 us -> none
    pallas_call x0 -> x1, Pallas kernels: none -> 1.91 us  [body(): return tuple(store(*done))]
    pallas_call x1, Pallas kernels: 20.8 us -> 20.2 us  [body(): call(query, key_in, value, grad_out, filt, *(jnp.asarray(t) for t in full))]
where the time goes in v2:
time: 22.9 us; the launch traced here: 22.8 us
  Pallas kernels  22.1 us (97%)
  between operations  0.64 us (3%)
    pallas_call x1, Pallas kernels, body(): call(query, key_in, value, grad_out, filt, *(jnp.asarray(t) for t in full))  20.2 us
    pallas_call x1, Pallas kernels, body(): return tuple(store(*done))  1.91 us

profile of v2, /device:TPU:0, one launch (start us, length us, event | category | flops | bytes accessed | tf_op | source)
XLA Modules:
  0.0 22.8 jit_solution(5546938155282088338)
XLA Ops:
  0.6 20.2 %shard_map.128 = (f32[1,256,128]{2,1,0:T(8,128)}, f32[1,256,128]{2,1,0:T(8,128)}, f32[1,256,128]{2,1,0:T(8,128)}, f32[1,256,128]{2,1,0:T(8,128)}, f32[32,1024]{1,0:T(8,128)}) custom-call(f32[1,256,128]{2,1,0:T(8,128)} %q_hbm.1, f32[1,256,128]{2,1,0:T(8,128)} %k_hbm.1, f32[1,256,128]{2,1,0:T(8,128)} %v_hbm.1, f32[1,256,128]{2,1,0:T(8,128)} %g_hbm.1, ...), custom_call_target="tpu_custom_call" | custom-call | tf_op jit(solution)/shard_map/pallas_call | solution.py:327
  20.9 1.9 %shard_map.129 = (f32[1,256,128]{2,1,0:T(8,128)}, f32[1,256,128]{2,1,0:T(8,128)}, f32[1,256,128]{2,1,0:T(8,128)}, f32[1,256,128]{2,1,0:T(8,128)}, f32[32,1024]{1,0:T(8,128)}) custom-call(f32[1,256,128]{2,1,0:T(8,128)} %get-tuple-element.10.refs_0_, f32[1,256,128]{2,1,0:T(8,128)} %get-tuple-element.11.refs_1_, f32[1,256,128]{2,1,0:T(8,128)} %get-tuple-element.12.refs_2_, ...), custom_call_target="tpu_custom_call" | custom-call | tf_op jit(solution)/shard_map/pallas_call | solution.py:336

commit v3 on v1

--- a/solution.py
+++ b/solution.py
@@ -14,6 +14,7 @@
 BLOCK = 128
 CHUNK = 8
 UNROLL = 8
+GRANT = 24 * 1024 * 1024
 
 
 def tables():
@@ -247,6 +248,15 @@
             back_copy(c, o).wait_send()
         for o in range(1, nd):
             filt_copy(c, o).wait_send()
+
+
+def writer(*refs):
+    sem = refs[10]
+    saves = [pltpu.make_async_copy(refs[at], refs[5 + at], sem.at[at]) for at in range(5)]
+    for save in saves:
+        save.start()
+    for save in saves:
+        save.wait()
 
 
 def body(query, key_in, value, grad_out, filt):
@@ -264,7 +274,7 @@
     call = pl.pallas_call(
         functools.partial(kernel, n, nd, ch, cc, scale),
         out_shape=[shape(query.shape)] * 4 + [shape(filt.shape)],
-        in_specs=[pl.BlockSpec(memory_space=pl.ANY)] * 9,
+        in_specs=[pl.BlockSpec(memory_space=pltpu.HBM)] * 9,
         out_specs=[pl.BlockSpec(memory_space=pltpu.VMEM)] * 5,
         scratch_shapes=[vmem(local)] * 4
         + [vmem(filt.shape)]
@@ -288,10 +298,20 @@
             dma((chunks, nd - 1)),
         ],
         compiler_params=pltpu.CompilerParams(
-            collective_id=0, has_side_effects=True, vmem_limit_bytes=24 * 1024 * 1024
+            collective_id=0, has_side_effects=True, vmem_limit_bytes=GRANT
         ),
     )
-    return tuple(call(query, key_in, value, grad_out, filt, *(jnp.asarray(t) for t in full)))
+    operands = [query, key_in, value, grad_out, filt] + [jnp.asarray(t) for t in full]
+    done = call(*(pltpu.with_memory_space_constraint(x, pltpu.HBM) for x in operands))
+    store = pl.pallas_call(
+        writer,
+        out_shape=[shape(query.shape)] * 4 + [shape(filt.shape)],
+        in_specs=[pl.BlockSpec(memory_space=pltpu.VMEM)] * 5,
+        out_specs=[pl.BlockSpec(memory_space=pltpu.HBM)] * 5,
+        scratch_shapes=[dma((5,))],
+        compiler_params=pltpu.CompilerParams(vmem_limit_bytes=GRANT),
+    )
+    return tuple(store(*done))
 
 
 def solution(mesh):

time: 32.9 us -> 21.3 us (0.65)
  local copies, waits for them, and re-layouts: 11.1 us -> 0 us
    unnamed x23 -> x0, local copies, waits for them, and re-layouts: 11.1 us -> none
    pallas_call x1 -> x2, Pallas kernels: 20.8 us -> 20.5 us  [the longest x1 19.6 us: body(): call(*(pltpu.with_memory_space_constraint(x, pltpu.HBM) for x in operands))]
where the time goes in v3:
time: 21.3 us; the launch traced here: 21.2 us
  Pallas kernels  20.5 us (96%)
  between operations  0.64 us (3%)
    pallas_call x1, Pallas kernels, body(): call(*(pltpu.with_memory_space_constraint(x, pltpu.HBM) for x in operands))  19.6 us
    pallas_call x1, Pallas kernels, body(): return tuple(store(*done))  0.87 us

profile of v3, /device:TPU:0, one launch (start us, length us, event | category | flops | bytes accessed | tf_op | source)
XLA Modules:
  0.0 21.2 jit_solution(17130161562717855252)
XLA Ops:
  0.6 19.6 %shard_map.128 = (f32[1,256,128]{2,1,0:T(8,128)S(1)}, f32[1,256,128]{2,1,0:T(8,128)S(1)}, f32[1,256,128]{2,1,0:T(8,128)S(1)}, f32[1,256,128]{2,1,0:T(8,128)S(1)}, f32[32,1024]{1,0:T(8,128)S(1)}) custom-call(f32[1,256,128]{2,1,0:T(8,128)} %q_hbm.1, f32[1,256,128]{2,1,0:T(8,128)} %k_hbm.1, f32[1,256,128]{2,1,0:T(8,128)} %v_hbm.1, f32[1,256,128]{2,1,0:T(8,128)} %g_hbm.1, ...), custom_call_target="tpu_custom_call" | custom-call | tf_op jit(solution)/shard_map/pallas_call | solution.py:305
  20.3 0.9 %shard_map.129 = (f32[1,256,128]{2,1,0:T(8,128)}, f32[1,256,128]{2,1,0:T(8,128)}, f32[1,256,128]{2,1,0:T(8,128)}, f32[1,256,128]{2,1,0:T(8,128)}, f32[32,1024]{1,0:T(8,128)}) custom-call(f32[1,256,128]{2,1,0:T(8,128)S(1)} %get-tuple-element.10.refs_0_, f32[1,256,128]{2,1,0:T(8,128)S(1)} %get-tuple-element.11.refs_1_, ...), custom_call_target="tpu_custom_call" | custom-call | tf_op jit(solution)/shard_map/pallas_call | solution.py:314

commit v4 on v3

--- a/solution.py
+++ b/solution.py
@@ -68,7 +68,15 @@
     me = lax.axis_index("seq")
     row = lax.axis_index("dp")
     chunks = ch // cc
-    offsets = sorted(range(1, n), key=lambda o: -min(o, n - o))
+    half = n // 2
+    offsets = range(1, n)
+    side = me // half * half
+
+    def partner(o):
+        if o <= half:
+            return lax.rem(side + half, n) + lax.rem(me - side + o - 1, half)
+        return side + lax.rem(me - side + o - half, half)
+
 
     loads = [
         pltpu.make_async_copy(src, dst, load_sem.at[at])
@@ -103,7 +111,7 @@
         recv[c, me] = send[me, c]
 
     def out_copy(c, o):
-        to = lax.rem(me + o, n)
+        to = partner(o)
         return pltpu.make_async_remote_copy(
             src_ref=send.at[to, c],
             dst_ref=recv.at[c, me],
@@ -114,7 +122,7 @@
         )
 
     def back_copy(c, o):
-        to = lax.rem(me + o, n)
+        to = partner(o)
         return pltpu.make_async_remote_copy(
             src_ref=ret.at[c, to],
             dst_ref=back.at[me, c],

time: 21.3 us -> 21.4 us (level)
  no operation moved by 1% of the time
where the time goes in v4:
time: 21.4 us; the launch traced here: 21.2 us
  Pallas kernels  20.6 us (96%)
  between operations  0.64 us (3%)
    pallas_call x1, Pallas kernels, body(): call(*(pltpu.with_memory_space_constraint(x, pltpu.HBM) for x in operands))  19.7 us
    pallas_call x1, Pallas kernels, body(): return tuple(store(*done))  0.87 us

profile of v4, /device:TPU:0, one launch (start us, length us, event | category | flops | bytes accessed | tf_op | source)
XLA Modules:
  0.0 21.2 jit_solution(9823694621249492266)
XLA Ops:
  0.6 19.7 %shard_map.128 = (f32[1,256,128]{2,1,0:T(8,128)S(1)}, f32[1,256,128]{2,1,0:T(8,128)S(1)}, f32[1,256,128]{2,1,0:T(8,128)S(1)}, f32[1,256,128]{2,1,0:T(8,128)S(1)}, f32[32,1024]{1,0:T(8,128)S(1)}) custom-call(f32[1,256,128]{2,1,0:T(8,128)} %q_hbm.1, f32[1,256,128]{2,1,0:T(8,128)} %k_hbm.1, f32[1,256,128]{2,1,0:T(8,128)} %v_hbm.1, f32[1,256,128]{2,1,0:T(8,128)} %g_hbm.1, ...), custom_call_target="tpu_custom_call" | custom-call | tf_op jit(solution)/shard_map/pallas_call | solution.py:313
  20.4 0.9 %shard_map.129 = (f32[1,256,128]{2,1,0:T(8,128)}, f32[1,256,128]{2,1,0:T(8,128)}, f32[1,256,128]{2,1,0:T(8,128)}, f32[1,256,128]{2,1,0:T(8,128)}, f32[32,1024]{1,0:T(8,128)}) custom-call(f32[1,256,128]{2,1,0:T(8,128)S(1)} %get-tuple-element.10.refs_0_, f32[1,256,128]{2,1,0:T(8,128)S(1)} %get-tuple-element.11.refs_1_, ...), custom_call_target="tpu_custom_call" | custom-call | tf_op jit(solution)/shard_map/pallas_call | solution.py:322
